TPU v7x, 512 devices: a whole 4x8x8 slice. The times are simulated.
512 devices in a mesh: fsdp: 32 (over y, z_hi), tp: 16 (over x, z_lo, core).
Axes of the slice: x: 4, y: 8, z: 8 (z_hi: 4, z_lo: 2; z = z_hi * 2 + z_lo), core: 2. Of those that a mesh axis runs over, the one named last changes fastest.
Arguments:
- acts: bfloat16 [8192, 4096], P('fsdp'), may hold values from -6 to 6
- cots: bfloat16 [8192, 14336], P('fsdp', 'tp'), may hold values from -6 to 6
- weight: bfloat16 [4096, 14336], P('fsdp', 'tp'), may hold values from -0.09375 to 0.09375
- basis_in: bfloat16 [32, 128, 128], P('fsdp'), may hold values from -0.5 to 0.5
- basis_out: bfloat16 [16, 896, 896], P('tp', 'fsdp'), may hold values from -0.1875 to 0.1875
- eigen_in: float32 [4096], P('fsdp'), may hold values from 0.2 to 5
- eigen_out: float32 [14336], P('tp'), may hold values from 0.2 to 5
- forget_rows: int32 [2048], P('fsdp'), may hold values from 0 to 255
- retain_rows: int32 [1024], P('fsdp'), may hold values from 0 to 255
Outputs:
- retained: bfloat16 [1024, 14336], P('fsdp', 'tp')
- back_grads: bfloat16 [1024, 4096], P('fsdp')
All inputs are finite; a program needn't handle non-finite values.
Results may differ from a plain program's by a relative error of at most 0.022.
Values may be sent and summed in bfloat16 or wider, within the bound.
A program may use at most 64 MiB of HBM per device.

v0:
```python
import jax
import jax.numpy as jnp
from jax import lax
from jax.sharding import PartitionSpec as P

damping = 0.1
step_size = 0.5


def shards(acts, cots, weight, basis_in, basis_out, eigen_in, eigen_out, forget_rows, retain_rows):
    fsdp_count = lax.axis_size("fsdp")
    forget_local = forget_rows.shape[0]
    forget_count = forget_local * fsdp_count
    row_count = weight.shape[0]
    col_count = weight.shape[1]
    in_blocks = basis_in.shape[0]
    in_order = basis_in.shape[1]
    forget_acts = jnp.take(acts, forget_rows, axis=0)
    forget_cots = jnp.take(cots, forget_rows, axis=0)
    basis_full = lax.all_gather(basis_out, "fsdp", axis=1, tiled=True)
    out_blocks = basis_full.shape[0]
    out_order = basis_full.shape[2]
    rotated_cots = (
        jnp.einsum(
            "tgi,gij->tgj",
            forget_cots.reshape(forget_local, out_blocks, out_order),
            basis_full,
            preferred_element_type=jnp.float32,
        )
        .reshape(forget_local, col_count)
        .astype(jnp.bfloat16)
    )
    feature_cols = lax.all_to_all(forget_acts, "fsdp", split_axis=1, concat_axis=0, tiled=True)
    rotated_acts = (
        jnp.einsum(
            "tbi,bij->tbj",
            feature_cols.reshape(forget_count, in_blocks, in_order),
            basis_in,
            preferred_element_type=jnp.float32,
        )
        .reshape(forget_count, row_count)
        .astype(jnp.bfloat16)
    )
    moments = (
        lax.dot_general(
            rotated_acts,
            lax.all_gather(rotated_cots, "fsdp", axis=0, tiled=True),
            (((0,), (0,)), ((), ())),
            preferred_element_type=jnp.float32,
        )
        / forget_count
    )
    damped = eigen_in[:, None] * eigen_out[None, :] + damping
    scaled = (moments / damped).astype(jnp.bfloat16)
    back_out = (
        jnp.einsum(
            "dgi,gji->dgj",
            scaled.reshape(row_count, out_blocks, out_order),
            basis_full,
            preferred_element_type=jnp.float32,
        )
        .reshape(row_count, col_count)
        .astype(jnp.bfloat16)
    )
    update = jnp.einsum(
        "bij,bjc->bic",
        basis_in,
        back_out.reshape(in_blocks, in_order, col_count),
        preferred_element_type=jnp.float32,
    ).reshape(row_count, col_count)
    new_weight = (weight.astype(jnp.float32) + step_size * update).astype(jnp.bfloat16)
    retain_acts = jnp.take(acts, retain_rows, axis=0)
    retain_cots = jnp.take(cots, retain_rows, axis=0)
    retain_cols = lax.all_to_all(retain_acts, "fsdp", split_axis=1, concat_axis=0, tiled=True)
    retained = lax.psum_scatter(
        jnp.dot(retain_cols, new_weight, preferred_element_type=jnp.float32).astype(jnp.bfloat16),
        "fsdp",
        scatter_dimension=0,
        tiled=True,
    )
    grad_cols = lax.dot_general(
        lax.all_gather(retain_cots, "fsdp", axis=0, tiled=True),
        new_weight,
        (((1,), (1,)), ((), ())),
        preferred_element_type=jnp.float32,
    )
    grad_summed = lax.psum(grad_cols.astype(jnp.bfloat16), "tp")
    back_grads = lax.all_to_all(grad_summed, "fsdp", split_axis=0, concat_axis=1, tiled=True)
    return (retained, back_grads)


def solution(mesh):
    placed = (
        P("fsdp", None),
        P("fsdp", "tp"),
        P("fsdp", "tp"),
        P("fsdp", None, None),
        P("tp", "fsdp", None),
        P("fsdp"),
        P("tp"),
        P("fsdp"),
        P("fsdp"),
    )
    return jax.shard_map(
        shards,
        mesh=mesh,
        in_specs=placed,
        out_specs=(P("fsdp", "tp"), P("fsdp", None)),
        check_vma=False,
    )
```

profile of v0, /device:TPU:2, one launch (start us, length us, event | category | flops | bytes accessed | tf_op | source)
XLA Modules:
  0.0 666.9 jit_solution(1411980744719282719)
XLA Ops:
  7.2 0.0 all-gather.4.cloned.1.call-start
  7.2 1.7 copy.25
  8.9 0.0 all-gather.4.cloned.1.call-update
  9.0 0.0 all-gather.6.cloned.1.call-start
  9.0 0.7 compare_select_fusion
  9.7 1.9 gather_fusion.2
  11.5 0.7 compare_and_fusion
  12.2 99.0 %all-gather.4.cloned.1.call-done = bf16[1,896,896]{2,0,1:T(2,128)(2,1)} async-done(((bf16[1,28,896]{2,0,1:T(2,128)(2,1)}), bf16[1,896,896]{2,0,1:T(2,128)(2,1)}) %all-gather.4.cloned.1.call-update) | async-done | bytes 1605648 | tf_op jit(solution)/shard_map/all_gather | solution.py:20
  111.2 3.0 fusion.16
  114.2 0.0 all-gather.8.cloned.1.call-start
  114.3 0.6 gather_fusion.3
  114.9 0.7 broadcast_select_fusion
  115.7 0.9 gather_fusion.1
  116.6 1.1 bitcast_select_fusion
  117.6 6.8 %all-to-all-start.1 = ((bf16[64,32,128]{2,0,1:T(8,128)(2,1)}), bf16[64,32,128]{2,0,1:T(8,128)(2,1)S(1)}, u32[]{:S(2)}, u32[]{:S(2)}) async-start(bf16[64,32,128]{2,0,1:T(8,128)(2,1)} %bitcast_select_fusion), calls=%async_computation.1 | async-start | bytes 1048576 | tf_op jit(solution)/shard_map/all_to_all | solution.py:33
  124.5 0.7 gather_fusion
  125.2 0.2 copy.23
  125.4 0.8 bitcast_select_fusion.1
  126.2 16.7 %all-to-all-done.1 = bf16[64,32,128]{2,0,1:T(8,128)(2,1)S(1)} async-done(((bf16[64,32,128]{2,0,1:T(8,128)(2,1)}), bf16[64,32,128]{2,0,1:T(8,128)(2,1)S(1)}, u32[]{:S(2)}, u32[]{:S(2)}) %all-to-all-start.1) | async-done | bytes 524320 | tf_op jit(solution)/shard_map/all_to_all | solution.py:33
  142.9 5.6 all-to-all-start
  148.6 0.0 all-reduce.2.cloned.1.call-start
  148.6 66.9 %all-gather.6.cloned.1.call-done = bf16[2048,896]{1,0:T(8,128)(2,1)} async-done(((bf16[64,896]{1,0:T(8,128)(2,1)}), bf16[2048,896]{1,0:T(8,128)(2,1)}) %all-gather.6.cloned.1.call-update) | async-done | bytes 3670032 | tf_op jit(solution)/shard_map/all_gather | solution.py:47
  215.6 3.0 fusion.13
  218.6 2.8 fusion.12
  221.4 78.9 %all-gather.8.cloned.1.call-done = bf16[1024,896]{1,0:T(8,128)(2,1)} async-done(((bf16[32,896]{1,0:T(8,128)(2,1)}), bf16[1024,896]{1,0:T(8,128)(2,1)}) %all-gather.8.cloned.1.call-update) | async-done | bytes 1835024 | tf_op jit(solution)/shard_map/all_gather | solution.py:82
  300.3 2.9 convolution_convert_fusion.2
  303.2 0.0 reduce-scatter.2.cloned.1.call-start
  303.2 1.9 convolution_convert_fusion.1
  305.1 116.9 %all-reduce.2.cloned.1.call-done = bf16[32,32,128]{2,1,0:T(8,128)(2,1)} async-done(((bf16[32,32,128]{2,1,0:T(8,128)(2,1)}), bf16[32,32,128]{2,1,0:T(8,128)(2,1)}) %all-reduce.2.cloned.1.call-update) | async-done | bytes 262160 | tf_op jit(solution)/shard_map/psum | solution.py:87
  422.1 25.1 %all_to_all.48 = bf16[32,32,128]{2,1,0:T(8,128)(2,1)S(1)} all-to-all(bf16[32,32,128]{2,1,0:T(8,128)(2,1)} %all-reduce.2.cloned.1.call-done), channel_id=1, replica_groups=mesh['fsdp'=32,'tp'=16] {'fsdp'}, dimensions={0} | all-to-all | bytes 524288 | tf_op jit(solution)/shard_map/all_to_all | solution.py:88
  447.1 0.7 copy_bitcast_fusion
  447.8 212.5 %reduce-scatter.2.cloned.1.call-done = bf16[32,896]{1,0:T(8,128)(2,1)} async-done(((bf16[1024,896]{1,0:T(8,128)(2,1)}), bf16[32,896]{1,0:T(8,128)(2,1)}) %reduce-scatter.2.cloned.1.call-update) | async-done | bytes 57360 | tf_op jit(solution)/shard_map/reduce_scatter | solution.py:75
  (23 shorter events, 0.1 us)
Async XLA Ops:
  7.2 108.5 %copy-start = (bf16[256,4096]{1,0:T(8,128)(2,1)S(1)}, bf16[256,4096]{1,0:T(8,128)(2,1)}, u32[]{:S(2)}) copy-start(bf16[256,4096]{1,0:T(8,128)(2,1)} %param.9) | copy-start | bytes 6291460
  7.2 107.1 %copy-start.1 = (bf16[256,896]{1,0:T(8,128)(2,1)S(1)}, bf16[256,896]{1,0:T(8,128)(2,1)}, u32[]{:S(2)}) copy-start(bf16[256,896]{1,0:T(8,128)(2,1)} %param.10) | copy-start | bytes 1376260
  7.2 107.0 %copy-start.5 = (s32[32]{0:T(128)S(1)}, s32[32]{0:T(128)}, u32[]{:S(2)}) copy-start(s32[32]{0:T(128)} %param.17) | copy-start | bytes 388
  7.2 104.0 %all-gather.4.cloned.1.call-start = ((), (), s32[]{:S(2)}) async-start(), calls=%async_computation.4 | async-start | bytes 3311616 | tf_op jit(solution)/shard_map/all_gather | solution.py:20
  9.0 206.6 %all-gather.6.cloned.1.call-start = ((), (), s32[]{:S(2)}) async-start(), calls=%async_computation.5 | async-start | bytes 3784704 | tf_op jit(solution)/shard_map/all_gather | solution.py:47
  114.2 186.1 %all-gather.8.cloned.1.call-start = ((), (), s32[]{:S(2)}) async-start(), calls=%async_computation.7 | async-start | bytes 1892352 | tf_op jit(solution)/shard_map/all_gather | solution.py:82
  116.5 8.7 %copy-start.2 = (bf16[128,896]{1,0:T(8,128)(2,1)S(1)}, bf16[128,896]{1,0:T(8,128)(2,1)}, u32[]{:S(2)}) copy-start(bf16[128,896]{1,0:T(8,128)(2,1)} %param.11) | copy-start | bytes 688132
  117.6 25.3 %all-to-all-start.1 = ((bf16[64,32,128]{2,0,1:T(8,128)(2,1)}), bf16[64,32,128]{2,0,1:T(8,128)(2,1)S(1)}, u32[]{:S(2)}, u32[]{:S(2)}) async-start(bf16[64,32,128]{2,0,1:T(8,128)(2,1)} %bitcast_select_fusion), calls=%async_computation.1 | async-start | bytes 1048576 | tf_op jit(solution)/shard_map/all_to_all | solution.py:33
  124.4 91.1 %copy-start.3 = (bf16[1,128,128]{2,1,0:T(8,128)(2,1)S(1)}, bf16[1,128,128]{2,1,0:T(8,128)(2,1)}, u32[]{:S(2)}) copy-start(bf16[1,128,128]{2,1,0:T(8,128)(2,1)} %param.12) | copy-start | bytes 98308
  124.5 91.1 %copy-start.4 = (f32[896]{0:T(1024)S(1)}, f32[896]{0:T(1024)}, u32[]{:S(2)}) copy-start(f32[896]{0:T(1024)} %param.15) | copy-start | bytes 10756
  124.5 91.1 %copy-start.6 = (f32[128]{0:T(128)S(1)}, f32[128]{0:T(128)}, u32[]{:S(2)}) copy-start(f32[128]{0:T(128)} %param.14) | copy-start | bytes 1540
  142.9 160.3 %all-to-all-start = ((bf16[32,32,128]{2,0,1:T(8,128)(2,1)}), bf16[32,32,128]{2,0,1:T(8,128)(2,1)S(1)}, u32[]{:S(2)}, u32[]{:S(2)}) async-start(bf16[32,32,128]{2,0,1:T(8,128)(2,1)} %bitcast_select_fusion.1), calls=%async_computation | async-start | bytes 524288 | tf_op jit(solution)/shard_map/all_to_all | solution.py:74
  148.6 273.5 %all-reduce.2.cloned.1.call-start = ((), (), s32[]{:S(2)}) async-start(), calls=%async_computation.8 | async-start | bytes 524288 | tf_op jit(solution)/shard_map/psum | solution.py:87
  303.2 357.2 %reduce-scatter.2.cloned.1.call-start = ((), (), s32[]{:S(2)}) async-start(), calls=%async_computation.6 | async-start | bytes 1892352 | tf_op jit(solution)/shard_map/reduce_scatter | solution.py:75
Sparse Core Ops, SparseCore 0:
  11.7 99.4 all-gather.3
  114.4 101.1 all-gather.5
  219.3 80.9 all-gather.7
  303.3 118.7 all-reduce.1
  427.6 232.6 reduce-scatter.1
where the time goes:
time: 667 us
  waiting for transfers between devices  591 us (89%)
  blocking collectives  25.1 us (4%)
  between operations  14 us (2%)
  matrix products  13.6 us (2%)
  starting transfers between devices  12.7 us (2%)
  local copies, waits for them, and re-layouts  6.69 us (1%)
    reduce_scatter x1, waiting for transfers between devices, shards(): lax.psum_scatter(jnp.dot(retain_cols, new_weight, preferred_element_type=...  213 us
    psum x1, waiting for transfers between devices, shards(): grad_summed = lax.psum(grad_cols.astype(jnp.bfloat16), 'tp')  117 us
    all_gather x1, waiting for transfers between devices, shards(): basis_full = lax.all_gather(basis_out, 'fsdp', axis=1, tiled=True)  99 us
    all_gather x1, waiting for transfers between devices, shards(): lax.all_gather(retain_cots, 'fsdp', axis=0, tiled=True)  78.9 us
    all_gather x1, waiting for transfers between devices, shards(): lax.all_gather(rotated_cots, 'fsdp', axis=0, tiled=True)  66.9 us
    all_to_all x1, blocking collectives, shards(): lax.all_to_all(grad_summed, 'fsdp', split_axis=0, concat_axis=1, tiled=True)  25.1 us
    all_to_all x1, waiting for transfers between devices, shards(): lax.all_to_all(forget_acts, 'fsdp', split_axis=1, concat_axis=0, tiled=True)  16.7 us
  transfers between devices with their start and end apart: 7, of which 6 were waited for; matrix products, arithmetic and copies ran while one was open for 3% of the time, Pallas kernels for 0%

commit v1 on v0

--- a/solution.py
+++ b/solution.py
@@ -85,7 +85,10 @@
         preferred_element_type=jnp.float32,
     )
     grad_summed = lax.psum(grad_cols.astype(jnp.bfloat16), "tp")
-    back_grads = lax.all_to_all(grad_summed, "fsdp", split_axis=0, concat_axis=1, tiled=True)
+    size = lax.axis_size("fsdp")
+    shards_2 = jnp.stack(jnp.split(grad_summed, size, axis=0), axis=0)
+    shards_2 = lax.all_to_all(shards_2, "fsdp", split_axis=0, concat_axis=0)
+    back_grads = jnp.concatenate(shards_2, axis=1)
     return (retained, back_grads)
 
 

time: 667 us -> 670 us (level)
  local copies, waits for them, and re-layouts: 6.69 us -> 29.2 us
  waiting for transfers between devices: 591 us -> 569 us
    reduce_scatter x1, waiting for transfers between devices: 213 us -> 191 us  [shards(): lax.psum_scatter(jnp.dot(retain_cols, new_weight, preferred_element_type=...]
    unnamed x16 -> x47, local copies, waits for them, and re-layouts: 1.9 us -> 23.7 us
  transfers between devices with their start and end apart: 7 -> 7, of which waited for: 6 -> 6; matrix products, arithmetic and copies ran while one was open for 3% -> 6% of each run, Pallas kernels for 0% -> 0%
where the time goes in v1:
time: 670 us; the launch traced here: 668 us
  waiting for transfers between devices  569 us (85%)
  local copies, waits for them, and re-layouts  29.2 us (4%)
  blocking collectives  25.2 us (4%)
  between operations  14 us (2%)
  matrix products  13.6 us (2%)
  starting transfers between devices  12.7 us (2%)
    reduce_scatter x1, waiting for transfers between devices, shards(): lax.psum_scatter(jnp.dot(retain_cols, new_weight, preferred_element_type=...  191 us
    psum x1, waiting for transfers between devices, shards(): grad_summed = lax.psum(grad_cols.astype(jnp.bfloat16), 'tp')  117 us
    all_gather x1, waiting for transfers between devices, shards(): basis_full = lax.all_gather(basis_out, 'fsdp', axis=1, tiled=True)  99 us
    all_gather x1, waiting for transfers between devices, shards(): lax.all_gather(retain_cots, 'fsdp', axis=0, tiled=True)  78.9 us
    all_gather x1, waiting for transfers between devices, shards(): lax.all_gather(rotated_cots, 'fsdp', axis=0, tiled=True)  66.9 us
    all_to_all x1, blocking collectives, shards(): shards_2 = lax.all_to_all(shards_2, 'fsdp', split_axis=0, concat_axis=0)  25.2 us
    unnamed x47, local copies, waits for them, and re-layouts  23.7 us
    all_to_all x1, waiting for transfers between devices, shards(): lax.all_to_all(forget_acts, 'fsdp', split_axis=1, concat_axis=0, tiled=True)  16.7 us
  transfers between devices with their start and end apart: 7, of which 6 were waited for; matrix products, arithmetic and copies ran while one was open for 6% of the time, Pallas kernels for 0%

profile of v1, /device:TPU:2, one launch (start us, length us, event | category | flops | bytes accessed | tf_op | source)
XLA Modules:
  0.0 667.7 jit_solution(9526452176423979905)
XLA Ops:
  7.2 1.7 copy.24
  9.7 1.9 gather_fusion.2
  12.2 99.0 %all-gather.4.cloned.1.call-done = bf16[1,896,896]{2,0,1:T(2,128)(2,1)} async-done(((bf16[1,28,896]{2,0,1:T(2,128)(2,1)}), bf16[1,896,896]{2,0,1:T(2,128)(2,1)}) %all-gather.4.cloned.1.call-update) | async-done | bytes 1605648 | tf_op jit(solution)/shard_map/all_gather | solution.py:20
  111.2 3.0 fusion.16
  114.9 0.7 broadcast_select_fusion
  115.7 0.9 gather_fusion.1
  116.6 1.1 bitcast_select_fusion
  117.6 6.8 %all-to-all-start.1 = ((bf16[64,32,128]{2,0,1:T(8,128)(2,1)}), bf16[64,32,128]{2,0,1:T(8,128)(2,1)S(1)}, u32[]{:S(2)}, u32[]{:S(2)}) async-start(bf16[64,32,128]{2,0,1:T(8,128)(2,1)} %bitcast_select_fusion), calls=%async_computation.1 | async-start | bytes 1048576 | tf_op jit(solution)/shard_map/all_to_all | solution.py:33
  124.5 0.7 gather_fusion
  125.4 0.8 bitcast_select_fusion.1
  126.2 16.7 %all-to-all-done.1 = bf16[64,32,128]{2,0,1:T(8,128)(2,1)S(1)} async-done(((bf16[64,32,128]{2,0,1:T(8,128)(2,1)}), bf16[64,32,128]{2,0,1:T(8,128)(2,1)S(1)}, u32[]{:S(2)}, u32[]{:S(2)}) %all-to-all-start.1) | async-done | bytes 524320 | tf_op jit(solution)/shard_map/all_to_all | solution.py:33
  142.9 5.6 all-to-all-start
  148.6 66.9 %all-gather.6.cloned.1.call-done = bf16[2048,896]{1,0:T(8,128)(2,1)} async-done(((bf16[64,896]{1,0:T(8,128)(2,1)}), bf16[2048,896]{1,0:T(8,128)(2,1)}) %all-gather.6.cloned.1.call-update) | async-done | bytes 3670032 | tf_op jit(solution)/shard_map/all_gather | solution.py:47
  215.6 3.0 fusion.13
  218.6 2.8 fusion.12
  221.4 78.9 %all-gather.8.cloned.1.call-done = bf16[1024,896]{1,0:T(8,128)(2,1)} async-done(((bf16[32,896]{1,0:T(8,128)(2,1)}), bf16[1024,896]{1,0:T(8,128)(2,1)}) %all-gather.8.cloned.1.call-update) | async-done | bytes 1835024 | tf_op jit(solution)/shard_map/all_gather | solution.py:82
  300.3 2.9 convolution_convert_fusion.2
  303.2 1.9 convolution_convert_fusion.1
  305.1 116.9 %all-reduce.2.cloned.1.call-done = bf16[1024,128]{1,0:T(8,128)(2,1)} async-done(((bf16[1024,128]{1,0:T(8,128)(2,1)}), bf16[1024,128]{1,0:T(8,128)(2,1)}) %all-reduce.2.cloned.1.call-update) | async-done | bytes 262160 | tf_op jit(solution)/shard_map/psum | solution.py:87
  422.8 0.7 constant_dynamic-update-slice_fusion.30
  423.5 0.7 constant_dynamic-update-slice_fusion.29
  424.9 0.7 constant_dynamic-update-slice_fusion.27
  425.6 0.7 constant_dynamic-update-slice_fusion.26
  426.3 0.7 constant_dynamic-update-slice_fusion.25
  427.0 0.7 constant_dynamic-update-slice_fusion.24
  428.4 0.7 constant_dynamic-update-slice_fusion.22
  429.1 0.7 constant_dynamic-update-slice_fusion.21
  429.8 0.7 constant_dynamic-update-slice_fusion.20
  430.5 0.7 constant_dynamic-update-slice_fusion.19
  444.6 25.2 %all_to_all.34 = bf16[32,32,128]{2,1,0:T(8,128)(2,1)S(1)} all-to-all(bf16[32,32,128]{2,1,0:T(8,128)(2,1)S(1)} %constant_dynamic-update-slice_fusion), channel_id=1, replica_groups=mesh['fsdp'=32,'tp'=16] {'fsdp'}, dimensions={0} | all-to-all | bytes 524288 | tf_op jit(solution)/shard_map/all_to_all | solution.py:90
  469.7 0.7 copy_bitcast_fusion
  470.4 190.7 %reduce-scatter.2.cloned.1.call-done = bf16[32,896]{1,0:T(8,128)(2,1)} async-done(((bf16[1024,896]{1,0:T(8,128)(2,1)}), bf16[32,896]{1,0:T(8,128)(2,1)}) %reduce-scatter.2.cloned.1.call-update) | async-done | bytes 57360 | tf_op jit(solution)/shard_map/reduce_scatter | solution.py:75
  (55 shorter events, 18.0 us)
Async XLA Ops:
  7.2 108.5 %copy-start = (bf16[256,4096]{1,0:T(8,128)(2,1)S(1)}, bf16[256,4096]{1,0:T(8,128)(2,1)}, u32[]{:S(2)}) copy-start(bf16[256,4096]{1,0:T(8,128)(2,1)} %param.9) | copy-start | bytes 6291460
  7.2 107.1 %copy-start.1 = (bf16[256,896]{1,0:T(8,128)(2,1)S(1)}, bf16[256,896]{1,0:T(8,128)(2,1)}, u32[]{:S(2)}) copy-start(bf16[256,896]{1,0:T(8,128)(2,1)} %param.10) | copy-start | bytes 1376260
  7.2 107.0 %copy-start.5 = (s32[32]{0:T(128)S(1)}, s32[32]{0:T(128)}, u32[]{:S(2)}) copy-start(s32[32]{0:T(128)} %param.17) | copy-start | bytes 388
  7.2 104.0 %all-gather.4.cloned.1.call-start = ((), (), s32[]{:S(2)}) async-start(), calls=%async_computation.4 | async-start | bytes 3311616 | tf_op jit(solution)/shard_map/all_gather | solution.py:20
  9.0 206.6 %all-gather.6.cloned.1.call-start = ((), (), s32[]{:S(2)}) async-start(), calls=%async_computation.5 | async-start | bytes 3784704 | tf_op jit(solution)/shard_map/all_gather | solution.py:47
  114.2 186.1 %all-gather.8.cloned.1.call-start = ((), (), s32[]{:S(2)}) async-start(), calls=%async_computation.7 | async-start | bytes 1892352 | tf_op jit(solution)/shard_map/all_gather | solution.py:82
  116.5 8.7 %copy-start.2 = (bf16[128,896]{1,0:T(8,128)(2,1)S(1)}, bf16[128,896]{1,0:T(8,128)(2,1)}, u32[]{:S(2)}) copy-start(bf16[128,896]{1,0:T(8,128)(2,1)} %param.11) | copy-start | bytes 688132
  117.6 25.3 %all-to-all-start.1 = ((bf16[64,32,128]{2,0,1:T(8,128)(2,1)}), bf16[64,32,128]{2,0,1:T(8,128)(2,1)S(1)}, u32[]{:S(2)}, u32[]{:S(2)}) async-start(bf16[64,32,128]{2,0,1:T(8,128)(2,1)} %bitcast_select_fusion), calls=%async_computation.1 | async-start | bytes 1048576 | tf_op jit(solution)/shard_map/all_to_all | solution.py:33
  124.4 91.1 %copy-start.3 = (bf16[1,128,128]{2,1,0:T(8,128)(2,1)S(1)}, bf16[1,128,128]{2,1,0:T(8,128)(2,1)}, u32[]{:S(2)}) copy-start(bf16[1,128,128]{2,1,0:T(8,128)(2,1)} %param.12) | copy-start | bytes 98308
  124.5 91.1 %copy-start.4 = (f32[896]{0:T(1024)S(1)}, f32[896]{0:T(1024)}, u32[]{:S(2)}) copy-start(f32[896]{0:T(1024)} %param.15) | copy-start | bytes 10756
  124.5 91.1 %copy-start.6 = (f32[128]{0:T(128)S(1)}, f32[128]{0:T(128)}, u32[]{:S(2)}) copy-start(f32[128]{0:T(128)} %param.14) | copy-start | bytes 1540
  142.9 160.3 %all-to-all-start = ((bf16[32,32,128]{2,0,1:T(8,128)(2,1)}), bf16[32,32,128]{2,0,1:T(8,128)(2,1)S(1)}, u32[]{:S(2)}, u32[]{:S(2)}) async-start(bf16[32,32,128]{2,0,1:T(8,128)(2,1)} %bitcast_select_fusion.1), calls=%async_computation | async-start | bytes 524288 | tf_op jit(solution)/shard_map/all_to_all | solution.py:74
  148.6 273.5 %all-reduce.2.cloned.1.call-start = ((), (), s32[]{:S(2)}) async-start(), calls=%async_computation.8 | async-start | bytes 524288 | tf_op jit(solution)/shard_map/psum | solution.py:87
  303.2 358.0 %reduce-scatter.2.cloned.1.call-start = ((), (), s32[]{:S(2)}) async-start(), calls=%async_computation.6 | async-start | bytes 1892352 | tf_op jit(solution)/shard_map/reduce_scatter | solution.py:75
Sparse Core Ops, SparseCore 0:
  11.7 99.4 all-gather.3
  114.4 101.1 all-gather.5
  219.3 80.9 all-gather.7
  303.3 118.7 all-reduce.1
  427.6 233.4 reduce-scatter.1
